TPU v7x, 32 devices: a whole 2x2x4 slice. The times are simulated.
32 devices in a mesh: sec: 4 (over y, core), blk: 2 (over x), gy: 4 (over z).
Axes of the slice: x: 2, y: 2, z: 4, core: 2. Of those that a mesh axis runs over, the one named last changes fastest.
Arguments:
- normalized_kelvin: float32 [32, 64, 512], P('blk', 'gy', 'sec'), may hold values from 0.6 to 2
- co2_molar_part: float32 [32, 64, 512], P('blk', 'gy', 'sec'), may hold values from 0.02 to 0.2
- h2o_molar_part: float32 [32, 64, 512], P('blk', 'gy', 'sec'), may hold values from 0.02 to 0.25
- particulate_scaled: float32 [32, 64, 512], P('blk', 'gy', 'sec'), may hold values from 0.01 to 1
- region_local_subgrids: int32 [4, 2, 4, 512], P('sec', 'blk', 'gy'), may hold values from 0 to 511, each once within a row
- entry_target_tile: int32 [64, 5], P(('sec', 'blk', 'gy')), may hold values from 0 to 63, as said below
- nonempty_entries_per_strip: int32 [64], P(('sec', 'blk', 'gy')), may hold values from 1 to 5, as said below
- transfer_matrix_tiles: bfloat16 [64, 5, 256, 256], P(('sec', 'blk', 'gy')), may hold values from -0.15625 to 0.15625
Outputs:
- temperature_new: float32 [32, 64, 512], P('blk', 'gy', 'sec')
- carbon_dioxide_new: float32 [32, 64, 512], P('blk', 'gy', 'sec')
- water_new: float32 [32, 64, 512], P('blk', 'gy', 'sec')
- soot_new: float32 [32, 64, 512], P('blk', 'gy', 'sec')
- source: float32 [32, 64, 512], P('blk', 'gy', 'sec')
Inputs may be any that keep to these rules, and one draw needn't show every extreme that they name: `region_local_subgrids`: each device's row is a permutation of its 512 boxes. `entry_target_tile`: slot 0 of block row r names r itself; slots at or beyond the row's count are not read. `nonempty_entries_per_strip`: some block row has 5 live slots and some has 1.
All inputs are finite; a program needn't handle non-finite values.
Results may differ from a plain program's by a relative error of at most 0.0018.
Values may be sent and summed in bfloat16 or wider, within the bound.
A program may use at most 64 MiB of HBM per device.

v0:
```python
import functools

import jax
import jax.numpy as jnp
from jax import lax
from jax.experimental import pallas as pl
from jax.experimental.pallas import tpu as pltpu
from jax.sharding import PartitionSpec as P

BOX = 4
AXES = ("sec", "blk", "gy")

diffusion_rates = (0.12, 0.1, 0.1, 0.02)
vapour_attenuation_rate = (0.4, 1.6, 6.4, 25.6)
mixture_share_offset = (0.3, 0.25, 0.2, 0.15)
mixture_share_slope = (-0.05, 0.02, 0.03, 0.01)
particulate_attenuation_rate = 1.5
radiance_multiplier = 0.05
heating_rate = 0.1

SHARE_OFFSET = sum(mixture_share_offset)
SHARE_SLOPE = sum(mixture_share_slope)
VAPOUR_OFFSET = sum(b * k for b, k in zip(mixture_share_offset, vapour_attenuation_rate))
VAPOUR_SLOPE = sum(c * k for c, k in zip(mixture_share_slope, vapour_attenuation_rate))

MESH = pl.DeviceIdType.MESH
NT = (((1,), (1,)), ((), ()))
TN = (((0,), (0,)), ((), ()))


def iota(shape, dim):
    return lax.broadcasted_iota(jnp.int32, shape, dim)


def group_sum(value, axis):
    size = value.shape[axis]
    place = iota(value.shape, axis)
    for step in (1, 2):
        above = pltpu.roll(value, size - step, axis)
        below = pltpu.roll(value, step, axis)
        value = value + jnp.where((place & step) == 0, above, below)
    return value


def kernel(
    dims,
    counts,
    kelvin_hbm,
    co2_hbm,
    h2o_hbm,
    soot_hbm,
    order_hbm,
    tile_hbm,
    live_hbm,
    matrix_hbm,
    *rest,
):
    done = rest[0]
    (
        fields,
        order_ref,
        matrix,
        gathered,
        z_out,
        y_out,
        x_out,
        z_in,
        y_in,
        x_in,
        tile_ref,
        live_ref,
        in_sem,
        face_send,
        face_recv,
        send_sem,
        recv_sem,
    ) = rest[1:]
    cz, cy, cx = dims
    n_sec, n_blk, n_gy = counts
    cells = cz * cy
    rows = matrix.shape[0]
    slots = matrix.shape[1]
    zones = order_ref.shape[1]
    zone = zones // rows
    n_plane = n_blk * n_gy
    sec, blk, gy = (lax.axis_index(a) for a in AXES)
    plane = blk * n_gy + gy
    me = sec * n_plane + plane
    n_all = n_sec * n_plane

    copies = [
        pltpu.make_async_copy(src, fields.at[i], in_sem.at[i])
        for i, src in enumerate((kelvin_hbm, co2_hbm, h2o_hbm, soot_hbm))
    ]
    copies.append(pltpu.make_async_copy(order_hbm, order_ref, in_sem.at[4]))
    copies.append(pltpu.make_async_copy(matrix_hbm, matrix, in_sem.at[5]))
    copies.append(pltpu.make_async_copy(tile_hbm, tile_ref, in_sem.at[6]))
    copies.append(pltpu.make_async_copy(live_hbm, live_ref, in_sem.at[7]))
    for copy in copies:
        copy.start()

    def plane_peer(i):
        flat = lax.rem(me + i, n_all)
        return {
            "sec": lax.div(flat, n_plane),
            "blk": lax.rem(lax.div(flat, n_gy), n_blk),
            "gy": lax.rem(flat, n_gy),
        }

    def each(count, body):
        if count <= 32:
            for i in range(1, count):
                body(i)
        else:
            lax.fori_loop(1, count, lambda i, c: (body(i), c)[1], 0)

    barrier = pltpu.get_barrier_semaphore()
    each(
        n_all,
        lambda i: pl.semaphore_signal(
            barrier, inc=1, device_id=plane_peer(i), device_id_type=MESH
        ),
    )

    places = (("sec", sec, n_sec), ("blk", blk, n_blk), ("gy", gy, n_gy))
    landing = (x_in, z_in, y_in)
    leaving = (x_out, z_out, y_out)
    for (_, at, size), land in zip(places, landing):
        for side, edge in ((0, 0), (1, size - 1)):

            @pl.when(at == edge)
            def _(land=land, side=side):
                land[side] = jnp.zeros(land.shape[1:], land.dtype)

    copies[4].wait()
    order = order_ref[...]
    across = cx // BOX
    x_shape = (cx, zones)
    r_shape = (cells // BOX, zones)
    x_at = iota(x_shape, 0)
    r_at = iota(r_shape, 0)
    same_x = lax.rem(order, across) == lax.div(x_at, BOX)
    box_row = lax.div(r_at, cy) * (cy // BOX) + lax.div(lax.rem(r_at, cy), BOX)
    same_r = lax.div(order, across) == box_row
    pick_x = jnp.where(same_x & (lax.rem(x_at, BOX) == 0), 1.0, 0.0).astype(jnp.bfloat16)
    pick_r = same_r & (lax.rem(r_at, BOX) == 0)
    for copy in copies[:4]:
        copy.wait()

    kelvin = fields[0]
    vapour = fields[1] + fields[2]
    soot_kelvin = fields[3] * kelvin
    share = vapour * (VAPOUR_OFFSET + VAPOUR_SLOPE * kelvin) + (
        particulate_attenuation_rate * soot_kelvin * (SHARE_OFFSET + SHARE_SLOPE * kelvin)
    )
    squared = kelvin * kelvin
    emission = radiance_multiplier * (squared * squared) * share
    slabs = emission.reshape(cz // BOX, BOX, cy, cx)
    slabs = (slabs[:, 0] + slabs[:, 1] + slabs[:, 2] + slabs[:, 3]).reshape(cells // BOX, cx)
    box_mean = group_sum(group_sum(slabs, 0), 1) * (1.0 / (BOX * BOX * BOX))

    by_row = jnp.dot(box_mean.astype(jnp.bfloat16), pick_x, preferred_element_type=jnp.float32)
    emitted = jnp.sum(jnp.where(pick_r, by_row, 0.0), axis=0, keepdims=True)
    for r in range(rows):
        gathered[me * rows + r] = emitted[:, r * zone : (r + 1) * zone]

    lane = iota((cells, cx), 1)
    packed = jnp.zeros((cells, cx), jnp.float32)
    for f in range(4):
        field = fields.at[f]
        z_out[0, f] = field[pl.ds(0, cy), :]
        z_out[1, f] = field[pl.ds(cells - cy, cy), :]
        y_out[0, f] = field[pl.ds(0, cz, stride=cy), :]
        y_out[1, f] = field[pl.ds(cy - 1, cz, stride=cy), :]
        packed = jnp.where((lane >> 1) == f, pltpu.roll(field[...], 2 * f + 1, 1), packed)
    x_out[...] = jnp.transpose(packed)[:8]

    pl.semaphore_wait(barrier, n_all - 1)

    def push(start, length, peer, stage):
        block = gathered.at[pl.ds(start, length)]
        pltpu.make_async_remote_copy(
            src_ref=block,
            dst_ref=block,
            send_sem=send_sem.at[stage],
            recv_sem=recv_sem.at[stage],
            device_id=peer,
            device_id_type=MESH,
        ).start()

    def settle(length, sem):
        block = gathered.at[pl.ds(0, length)]
        pltpu.make_async_copy(block, block, sem).wait()

    each(n_all, lambda i: push(me * rows, rows, plane_peer(i), 0))

    def face(which, side):
        axis, at, _ = places[which]
        source = x_out if which == 0 else leaving[which].at[side]
        return pltpu.make_async_remote_copy(
            src_ref=source,
            dst_ref=landing[which].at[1 - side],
            send_sem=face_send.at[which, side],
            recv_sem=face_recv.at[which, 1 - side],
            device_id={axis: at + (2 * side - 1)},
            device_id_type=MESH,
        )

    def has(which, side):
        _, at, size = places[which]
        return at > 0 if side == 0 else at < size - 1

    for which in (1, 2, 0):
        for side in (0, 1):

            @pl.when(has(which, side))
            def _(which=which, side=side):
                face(which, side).start()

    place = iota((cells, cx), 0)
    y_place = lax.rem(place, cy)
    for f in range(4):
        value = fields[f]
        total = jnp.where(place >= cy, pltpu.roll(value, cy, 0), 0.0)
        total += jnp.where(place < cells - cy, pltpu.roll(value, cells - cy, 0), 0.0)
        total += jnp.where(y_place > 0, pltpu.roll(value, 1, 0), 0.0)
        total += jnp.where(y_place < cy - 1, pltpu.roll(value, cells - 1, 0), 0.0)
        total += jnp.where(lane > 0, pltpu.roll(value, 1, 1), 0.0)
        total += jnp.where(lane < cx - 1, pltpu.roll(value, cx - 1, 1), 0.0)
        done[f] = value + diffusion_rates[f] * (total - 6.0 * value)

    for which in (0, 1, 2):
        for side in (0, 1):

            @pl.when(has(which, side))
            def _(which=which, side=side):
                face(which, 1 - side).wait_recv()

    shape = (32, 4 * cx)
    row, column = iota(shape, 0) & 15, iota(shape, 1)
    chosen = ((row < 8) & (column == (row >> 1) * cx) & ((row & 1) == 0)) | (
        (row >= 8) & (column == ((row - 8) >> 1) * cx + cx - 1) & ((row & 1) == 1)
    )
    sides = jnp.concatenate([x_in[0], x_in[1]], axis=0)
    upper = sides.astype(jnp.bfloat16).astype(jnp.float32)
    x_add = lax.dot_general(
        jnp.concatenate([upper, sides - upper], axis=0),
        jnp.where(chosen, 1.0, 0.0),
        TN,
        preferred_element_type=jnp.float32,
    )
    for f in (1, 2, 3, 0):
        rate = diffusion_rates[f]
        out = done.at[f]
        out[...] += rate * x_add[:, f * cx : (f + 1) * cx]
        out[pl.ds(0, cy), :] += rate * z_in[0, f]
        out[pl.ds(cells - cy, cy), :] += rate * z_in[1, f]
        out[pl.ds(0, cz, stride=cy), :] += rate * y_in[0, f]
        out[pl.ds(cy - 1, cz, stride=cy), :] += rate * y_in[1, f]

    spread_x = jnp.where(same_x, 1.0, 0.0).astype(jnp.bfloat16)
    for copy in copies[5:]:
        copy.wait()
    settle((n_all - 1) * rows, recv_sem.at[0])

    absorbed = []
    for r in range(rows):
        total = jnp.zeros((1, zone), jnp.float32)
        for k in range(slots):
            tile = jnp.clip(tile_ref[r, k], 0, gathered.shape[0] - 1)
            picked = jnp.where(k < live_ref[r], gathered[tile], 0.0).astype(jnp.bfloat16)
            total += lax.dot_general(picked, matrix[r, k], NT, preferred_element_type=jnp.float32)
        absorbed.append(total)
    absorbed = jnp.concatenate(absorbed, axis=1)
    high = absorbed.astype(jnp.bfloat16).astype(jnp.float32)
    low = absorbed - high
    both = jnp.concatenate(
        [jnp.where(same_r, high, 0.0), jnp.where(same_r, low, 0.0)], axis=0
    ).astype(jnp.bfloat16)
    carried = lax.dot_general(both, spread_x, NT, preferred_element_type=jnp.float32)
    net = carried[: cells // BOX] + carried[cells // BOX :] - box_mean
    source = jnp.broadcast_to(
        net.reshape(cz // BOX, 1, cy, cx), (cz // BOX, BOX, cy, cx)
    ).reshape(cells, cx)
    done[4] = source
    done[0] += heating_rate * source

    settle((n_all - 1) * rows, send_sem.at[0])
    for which in (0, 1, 2):
        for side in (0, 1):

            @pl.when(has(which, side))
            def _(which=which, side=side):
                face(which, side).wait_send()


def carry(source, *rest):
    outs, sem = rest[:5], rest[5]
    copies = [pltpu.make_async_copy(source.at[i], out, sem.at[i]) for i, out in enumerate(outs)]
    for copy in copies:
        copy.start()
    for copy in copies:
        copy.wait()


def solution(mesh):
    counts = tuple(mesh.shape[a] for a in AXES)

    def local(kelvin, co2, h2o, soot, order, tiles, live, matrix):
        dims = kelvin.shape
        cz, cy, cx = dims
        cells = cz * cy
        rows = matrix.shape[0]
        zone = matrix.shape[2]
        blocks = counts[0] * counts[1] * counts[2] * rows
        flat = [a.reshape(cells, cx) for a in (kelvin, co2, h2o, soot)]
        order = order.reshape(1, -1)
        anywhere = pl.BlockSpec(memory_space=pl.ANY)
        f32 = jnp.float32
        done = pl.pallas_call(
            functools.partial(kernel, dims, counts),
            out_shape=pltpu.VMEM((5, cells, cx), f32),
            in_specs=[anywhere] * 8,
            out_specs=pl.BlockSpec(memory_space=pltpu.VMEM),
            scratch_shapes=[
                pltpu.VMEM((4, cells, cx), f32),
                pltpu.VMEM(order.shape, jnp.int32),
                pltpu.VMEM(matrix.shape, matrix.dtype),
                pltpu.VMEM((blocks, 1, zone), f32),
                pltpu.VMEM((2, 4, cy, cx), f32),
                pltpu.VMEM((2, 4, cz, cx), f32),
                pltpu.VMEM((8, cells), f32),
                pltpu.VMEM((2, 4, cy, cx), f32),
                pltpu.VMEM((2, 4, cz, cx), f32),
                pltpu.VMEM((2, 8, cells), f32),
                pltpu.SMEM(tiles.shape, tiles.dtype),
                pltpu.SMEM(live.shape, live.dtype),
                pltpu.SemaphoreType.DMA((8,)),
                pltpu.SemaphoreType.DMA((3, 2)),
                pltpu.SemaphoreType.DMA((3, 2)),
                pltpu.SemaphoreType.DMA((2,)),
                pltpu.SemaphoreType.DMA((2,)),
            ],
            compiler_params=pltpu.CompilerParams(collective_id=0, has_side_effects=True),
        )(*flat, order, tiles, live, matrix)
        outs = pl.pallas_call(
            carry,
            out_shape=[jax.ShapeDtypeStruct((cells, cx), f32)] * 5,
            in_specs=[anywhere],
            out_specs=[anywhere] * 5,
            scratch_shapes=[
                pltpu.SemaphoreType.DMA((5,)),
            ],
            compiler_params=pltpu.CompilerParams(vmem_limit_bytes=4 << 20),
        )(done)
        return tuple(o.reshape(dims) for o in outs)

    cell = P("blk", "gy", "sec")
    block = P(AXES)
    return jax.shard_map(
        local,
        mesh=mesh,
        in_specs=(cell,) * 4 + (P("sec", "blk", "gy", None), P(AXES, None), block, P(AXES, None, None, None)),
        out_specs=(cell,) * 5,
        check_vma=False,
    )
```

profile of v0, /device:TPU:0, one launch (start us, length us, event | category | flops | bytes accessed | tf_op | source)
XLA Modules:
  0.0 13.2 jit_solution(8706548653333211912)
XLA Ops:
  0.6 11.7 %shard_map.119.source = f32[5,256,128]{2,1,0:T(8,128)S(1)} custom-call(f32[256,128]{1,0:T(8,128)} %bitcast.10, f32[256,128]{1,0:T(8,128)} %bitcast.11, f32[256,128]{1,0:T(8,128)} %bitcast.12, f32[256,128]{1,0:T(8,128)} %bitcast.13, s32[1,512]{1,0:T(1,128)} %bitcast.14, s32[2,5]{1,0:T(2,128)} %tile_hbm.1, s32[2]{0:T(128)} %live_hbm.1, ...), custom_call_target="tpu_custom_call" | custom-call | tf_op jit(solution)/shard_map/pallas_call | solution.py:320
  12.4 0.9 %shard_map.120 = (f32[256,128]{1,0:T(8,128)}, f32[256,128]{1,0:T(8,128)}, f32[256,128]{1,0:T(8,128)}, f32[256,128]{1,0:T(8,128)}, f32[256,128]{1,0:T(8,128)}) custom-call(f32[5,256,128]{2,1,0:T(8,128)S(1)} %shard_map.119.source), custom_call_target="tpu_custom_call" | custom-call | tf_op jit(solution)/shard_map/pallas_call | solution.py:346
where the time goes:
time: 13.4 us; the launch traced here: 13.2 us
  Pallas kernels  12.6 us (94%)
  between operations  0.64 us (5%)
    pallas_call x1, Pallas kernels, local(): pl.pallas_call(functools.partial(kernel, dims, counts), out_shape=pltpu.V...  11.7 us
    pallas_call x1, Pallas kernels, local(): pl.pallas_call(carry, out_shape=[jax.ShapeDtypeStruct((cells, cx), f32)]...  0.87 us

commit v1 on v0

--- a/solution.py
+++ b/solution.py
@@ -55,11 +55,10 @@
     matrix_hbm,
     *rest,
 ):
-    done = rest[0]
+    done, matrix, picked_out, mean_out, rows_out, spread_out = rest[:6]
     (
         fields,
         order_ref,
-        matrix,
         gathered,
         z_out,
         y_out,
@@ -74,7 +73,7 @@
         face_recv,
         send_sem,
         recv_sem,
-    ) = rest[1:]
+    ) = rest[6:]
     cz, cy, cx = dims
     n_sec, n_blk, n_gy = counts
     cells = cz * cy
@@ -96,7 +95,7 @@
     copies.append(pltpu.make_async_copy(matrix_hbm, matrix, in_sem.at[5]))
     copies.append(pltpu.make_async_copy(tile_hbm, tile_ref, in_sem.at[6]))
     copies.append(pltpu.make_async_copy(live_hbm, live_ref, in_sem.at[7]))
-    for copy in copies:
+    for copy in copies[:5] + copies[6:]:
         copy.start()
 
     def plane_peer(i):
@@ -107,20 +106,24 @@
             "gy": lax.rem(flat, n_gy),
         }
 
-    def each(count, body):
-        if count <= 32:
-            for i in range(1, count):
-                body(i)
+    def each(body):
+        if n_all <= 32:
+            for flat in range(n_all):
+
+                @pl.when(me != flat)
+                def _(flat=flat):
+                    body(
+                        {
+                            "sec": flat // n_plane,
+                            "blk": flat // n_gy % n_blk,
+                            "gy": flat % n_gy,
+                        }
+                    )
         else:
-            lax.fori_loop(1, count, lambda i, c: (body(i), c)[1], 0)
+            lax.fori_loop(1, n_all, lambda i, c: (body(plane_peer(i)), c)[1], 0)
 
     barrier = pltpu.get_barrier_semaphore()
-    each(
-        n_all,
-        lambda i: pl.semaphore_signal(
-            barrier, inc=1, device_id=plane_peer(i), device_id_type=MESH
-        ),
-    )
+    each(lambda peer: pl.semaphore_signal(barrier, inc=1, device_id=peer, device_id_type=MESH))
 
     places = (("sec", sec, n_sec), ("blk", blk, n_blk), ("gy", gy, n_gy))
     landing = (x_in, z_in, y_in)
@@ -142,10 +145,12 @@
     same_x = lax.rem(order, across) == lax.div(x_at, BOX)
     box_row = lax.div(r_at, cy) * (cy // BOX) + lax.div(lax.rem(r_at, cy), BOX)
     same_r = lax.div(order, across) == box_row
-    pick_x = jnp.where(same_x & (lax.rem(x_at, BOX) == 0), 1.0, 0.0).astype(jnp.bfloat16)
-    pick_r = same_r & (lax.rem(r_at, BOX) == 0)
+    spread_x = jnp.where(same_x, 1.0, 0.0).astype(jnp.bfloat16)
+    spread_out[...] = spread_x
+    rows_out[...] = jnp.where(same_r, 1.0, 0.0)
     for copy in copies[:4]:
         copy.wait()
+    copies[5].start()
 
     kelvin = fields[0]
     vapour = fields[1] + fields[2]
@@ -157,10 +162,14 @@
     emission = radiance_multiplier * (squared * squared) * share
     slabs = emission.reshape(cz // BOX, BOX, cy, cx)
     slabs = (slabs[:, 0] + slabs[:, 1] + slabs[:, 2] + slabs[:, 3]).reshape(cells // BOX, cx)
-    box_mean = group_sum(group_sum(slabs, 0), 1) * (1.0 / (BOX * BOX * BOX))
-
-    by_row = jnp.dot(box_mean.astype(jnp.bfloat16), pick_x, preferred_element_type=jnp.float32)
-    emitted = jnp.sum(jnp.where(pick_r, by_row, 0.0), axis=0, keepdims=True)
+    slabs = slabs * (1.0 / (BOX * BOX * BOX))
+    upper = slabs.astype(jnp.bfloat16)
+    lower = (slabs - upper.astype(jnp.float32)).astype(jnp.bfloat16)
+    by_row = jnp.dot(
+        jnp.concatenate([upper, lower], axis=0), spread_x, preferred_element_type=jnp.float32
+    )
+    by_row = by_row[: cells // BOX] + by_row[cells // BOX :]
+    emitted = jnp.sum(jnp.where(same_r, by_row, 0.0), axis=0, keepdims=True)
     for r in range(rows):
         gathered[me * rows + r] = emitted[:, r * zone : (r + 1) * zone]
 
@@ -192,7 +201,7 @@
         block = gathered.at[pl.ds(0, length)]
         pltpu.make_async_copy(block, block, sem).wait()
 
-    each(n_all, lambda i: push(me * rows, rows, plane_peer(i), 0))
+    each(lambda peer: push(me * rows, rows, peer, 0))
 
     def face(which, side):
         axis, at, _ = places[which]
@@ -217,6 +226,7 @@
             def _(which=which, side=side):
                 face(which, side).start()
 
+    mean_out[...] = group_sum(group_sum(slabs, 0), 1)
     place = iota((cells, cx), 0)
     y_place = lax.rem(place, cy)
     for f in range(4):
@@ -258,47 +268,63 @@
         out[pl.ds(0, cz, stride=cy), :] += rate * y_in[0, f]
         out[pl.ds(cy - 1, cz, stride=cy), :] += rate * y_in[1, f]
 
-    spread_x = jnp.where(same_x, 1.0, 0.0).astype(jnp.bfloat16)
     for copy in copies[5:]:
         copy.wait()
     settle((n_all - 1) * rows, recv_sem.at[0])
+
+    for r in range(rows):
+        for k in range(slots):
+            tile = jnp.clip(tile_ref[r, k], 0, gathered.shape[0] - 1)
+            picked_out[r, k] = jnp.where(k < live_ref[r], gathered[tile], 0.0)
+
+    settle((n_all - 1) * rows, send_sem.at[0])
+    for which in (0, 1, 2):
+        for side in (0, 1):
+
+            @pl.when(has(which, side))
+            def _(which=which, side=side):
+                face(which, side).wait_send()
+
+
+def finish(dims, swept, matrix, picked, box_mean, same_r, spread_x, *rest):
+    outs, heated, source_ref, sem = rest[:5], rest[5], rest[6], rest[7]
+    cz, cy, cx = dims
+    cells = cz * cy
+    rows, slots, zone, _ = matrix.shape
+    copies = [
+        pltpu.make_async_copy(source, out, sem.at[i])
+        for i, (source, out) in enumerate(
+            zip((heated, swept.at[1], swept.at[2], swept.at[3], source_ref), outs)
+        )
+    ]
+    for copy in copies[1:4]:
+        copy.start()
 
     absorbed = []
     for r in range(rows):
         total = jnp.zeros((1, zone), jnp.float32)
         for k in range(slots):
-            tile = jnp.clip(tile_ref[r, k], 0, gathered.shape[0] - 1)
-            picked = jnp.where(k < live_ref[r], gathered[tile], 0.0).astype(jnp.bfloat16)
-            total += lax.dot_general(picked, matrix[r, k], NT, preferred_element_type=jnp.float32)
+            total += lax.dot_general(
+                picked[r, k].astype(jnp.bfloat16),
+                matrix[r, k],
+                NT,
+                preferred_element_type=jnp.float32,
+            )
         absorbed.append(total)
     absorbed = jnp.concatenate(absorbed, axis=1)
     high = absorbed.astype(jnp.bfloat16).astype(jnp.float32)
     low = absorbed - high
-    both = jnp.concatenate(
-        [jnp.where(same_r, high, 0.0), jnp.where(same_r, low, 0.0)], axis=0
-    ).astype(jnp.bfloat16)
-    carried = lax.dot_general(both, spread_x, NT, preferred_element_type=jnp.float32)
-    net = carried[: cells // BOX] + carried[cells // BOX :] - box_mean
+    mask = same_r[...]
+    both = jnp.concatenate([mask * high, mask * low], axis=0).astype(jnp.bfloat16)
+    carried = lax.dot_general(both, spread_x[...], NT, preferred_element_type=jnp.float32)
+    net = carried[: cells // BOX] + carried[cells // BOX :] - box_mean[...]
     source = jnp.broadcast_to(
         net.reshape(cz // BOX, 1, cy, cx), (cz // BOX, BOX, cy, cx)
     ).reshape(cells, cx)
-    done[4] = source
-    done[0] += heating_rate * source
-
-    settle((n_all - 1) * rows, send_sem.at[0])
-    for which in (0, 1, 2):
-        for side in (0, 1):
-
-            @pl.when(has(which, side))
-            def _(which=which, side=side):
-                face(which, side).wait_send()
-
-
-def carry(source, *rest):
-    outs, sem = rest[:5], rest[5]
-    copies = [pltpu.make_async_copy(source.at[i], out, sem.at[i]) for i, out in enumerate(outs)]
-    for copy in copies:
-        copy.start()
+    source_ref[...] = source
+    copies[4].start()
+    heated[...] = swept[0] + heating_rate * source
+    copies[0].start()
     for copy in copies:
         copy.wait()
 
@@ -317,15 +343,24 @@
         order = order.reshape(1, -1)
         anywhere = pl.BlockSpec(memory_space=pl.ANY)
         f32 = jnp.float32
-        done = pl.pallas_call(
+        vmem = pl.BlockSpec(memory_space=pltpu.VMEM)
+        zones = order.shape[1]
+        slots = matrix.shape[1]
+        parts = pl.pallas_call(
             functools.partial(kernel, dims, counts),
-            out_shape=pltpu.VMEM((5, cells, cx), f32),
+            out_shape=[
+                pltpu.VMEM((4, cells, cx), f32),
+                pltpu.VMEM(matrix.shape, matrix.dtype),
+                pltpu.VMEM((rows, slots, 1, zone), f32),
+                pltpu.VMEM((cells // BOX, cx), f32),
+                pltpu.VMEM((cells // BOX, zones), f32),
+                pltpu.VMEM((cx, zones), jnp.bfloat16),
+            ],
             in_specs=[anywhere] * 8,
-            out_specs=pl.BlockSpec(memory_space=pltpu.VMEM),
+            out_specs=[vmem] * 6,
             scratch_shapes=[
                 pltpu.VMEM((4, cells, cx), f32),
                 pltpu.VMEM(order.shape, jnp.int32),
-                pltpu.VMEM(matrix.shape, matrix.dtype),
                 pltpu.VMEM((blocks, 1, zone), f32),
                 pltpu.VMEM((2, 4, cy, cx), f32),
                 pltpu.VMEM((2, 4, cz, cx), f32),
@@ -344,15 +379,17 @@
             compiler_params=pltpu.CompilerParams(collective_id=0, has_side_effects=True),
         )(*flat, order, tiles, live, matrix)
         outs = pl.pallas_call(
-            carry,
+            functools.partial(finish, dims),
             out_shape=[jax.ShapeDtypeStruct((cells, cx), f32)] * 5,
-            in_specs=[anywhere],
+            in_specs=[vmem] * 6,
             out_specs=[anywhere] * 5,
             scratch_shapes=[
+                pltpu.VMEM((cells, cx), f32),
+                pltpu.VMEM((cells, cx), f32),
                 pltpu.SemaphoreType.DMA((5,)),
             ],
-            compiler_params=pltpu.CompilerParams(vmem_limit_bytes=4 << 20),
-        )(done)
+            compiler_params=pltpu.CompilerParams(vmem_limit_bytes=16 << 20),
+        )(*parts)
         return tuple(o.reshape(dims) for o in outs)
 
     cell = P("blk", "gy", "sec")

time: 13.4 us -> 13 us (0.970)
  Pallas kernels: 12.6 us -> 12.2 us
    pallas_call x2, Pallas kernels: 12.6 us -> 12.2 us  [the longest x1 10.9 us: local(): pl.pallas_call(functools.partial(kernel, dims, counts), out_shape=[pltpu....]
where the time goes in v1:
time: 13 us; the launch traced here: 12.9 us
  Pallas kernels  12.2 us (94%)
  between operations  0.64 us (5%)
    pallas_call x1, Pallas kernels, local(): pl.pallas_call(functools.partial(kernel, dims, counts), out_shape=[pltpu....  10.9 us
    pallas_call x1, Pallas kernels, local(): pl.pallas_call(functools.partial(finish, dims), out_shape=[jax.ShapeDtype...  1.37 us

profile of v1, /device:TPU:0, one launch (start us, length us, event | category | flops | bytes accessed | tf_op | source)
XLA Modules:
  0.0 12.9 jit_solution(17401940100209872514)
XLA Ops:
  0.6 10.9 %shard_map.119 = (f32[4,256,128]{2,1,0:T(8,128)S(1)}, bf16[2,5,256,256]{3,2,1,0:T(8,128)(2,1)S(1)}, f32[2,5,1,256]{3,2,1,0:T(1,128)S(1)}, f32[64,128]{1,0:T(8,12...) custom-call(f32[256,128]{1,0:T(8,128)} %bitcast.10, f32[256,128]{1,0:T(8,128)} %bitcast.11, ...), custom_call_target="tpu_custom_call" | custom-call | tf_op jit(solution)/shard_map/pallas_call | solution.py:349
  11.5 1.4 %shard_map.120 = (f32[256,128]{1,0:T(8,128)}, f32[256,128]{1,0:T(8,128)}, f32[256,128]{1,0:T(8,128)}, f32[256,128]{1,0:T(8,128)}, f32[256,128]{1,0:T(8,128)}) custom-call(f32[4,256,128]{2,1,0:T(8,128)S(1)} %get-tuple-element.16.swept, bf16[2,5,256,256]{3,2,1,0:T(8,128)(2,1)S(1)} %get-tuple-element.17.matrix, f32[2,5,1,256]{3,2,1,0:T(1,128)S(1)} %get-tuple-element.18.picked, ...), custom_call_target="tpu_custom_call" | custom-call | tf_op jit(solution)/shard_map/pallas_call | solution.py:381

commit v2 on v1

--- a/solution.py
+++ b/solution.py
@@ -73,6 +73,7 @@
         face_recv,
         send_sem,
         recv_sem,
+        far_sem,
     ) = rest[6:]
     cz, cy, cx = dims
     n_sec, n_blk, n_gy = counts
@@ -98,34 +99,86 @@
     for copy in copies[:5] + copies[6:]:
         copy.start()
 
-    def plane_peer(i):
-        flat = lax.rem(me + i, n_all)
-        return {
-            "sec": lax.div(flat, n_plane),
-            "blk": lax.rem(lax.div(flat, n_gy), n_blk),
-            "gy": lax.rem(flat, n_gy),
-        }
-
-    def each(body):
+    level = n_sec * n_blk
+
+    def steps(sec, blk, gy):
+        return sec // 2 + blk + gy
+
+    def beside(peer):
+        away = [abs(peer[a] - at) for a, at in zip(AXES, (sec, blk, gy))]
+        return away[0] + away[1] + away[2] == 1
+
+    def each(chosen, body):
         if n_all <= 32:
-            for flat in range(n_all):
-
-                @pl.when(me != flat)
-                def _(flat=flat):
-                    body(
-                        {
-                            "sec": flat // n_plane,
-                            "blk": flat // n_gy % n_blk,
-                            "gy": flat % n_gy,
-                        }
-                    )
+            for r in range(n_all):
+                peer = {"sec": r % n_sec, "blk": r // n_sec % n_blk, "gy": r // level}
+
+                @pl.when(chosen(peer))
+                def _(peer=peer):
+                    body(peer)
         else:
-            lax.fori_loop(1, n_all, lambda i, c: (body(plane_peer(i)), c)[1], 0)
+
+            @pl.loop(0, n_all)
+            def _(r):
+                peer = {
+                    "sec": lax.rem(r, n_sec),
+                    "blk": lax.rem(lax.div(r, n_sec), n_blk),
+                    "gy": lax.div(r, level),
+                }
+
+                @pl.when(chosen(peer))
+                def _():
+                    body(peer)
+
+    def other(peer):
+        return (peer["sec"] * n_blk + peer["blk"]) * n_gy + peer["gy"] != me
+
+    def first(peer):
+        return jnp.asarray(steps(**peer) <= 1)
+
+    mine = steps(sec, blk, gy)
+    early = mine <= 1
+    last = mine == (n_sec - 1) // 2 + n_blk + n_gy - 2
+    n_first = sum(
+        a // 2 + b + c <= 1 for a in range(n_sec) for b in range(n_blk) for c in range(n_gy)
+    )
+
+    def both(a, b):
+        return jnp.logical_and(a, b)
+
+    def either(a, b):
+        return jnp.logical_or(a, b)
+
+    def greeted(peer):
+        return both(other(peer), either(early, either(~first(peer), beside(peer))))
+
+    def greet(sem):
+        return lambda peer: pl.semaphore_signal(
+            sem, inc=1, device_id=peer, device_id_type=MESH
+        )
 
     barrier = pltpu.get_barrier_semaphore()
-    each(lambda peer: pl.semaphore_signal(barrier, inc=1, device_id=peer, device_id_type=MESH))
+    each(greeted, greet(barrier))
 
     places = (("sec", sec, n_sec), ("blk", blk, n_blk), ("gy", gy, n_gy))
+    late = jnp.int32(0)
+    for axis, at, size in places:
+        for move, inside in ((-1, at > 0), (1, at < size - 1)):
+            there = dict(zip(AXES, (sec, blk, gy)))
+            there[axis] = at + move
+            late += both(inside, steps(**there) > 1).astype(jnp.int32)
+
+    def enter():
+        pl.semaphore_wait(barrier, jnp.where(early, n_first - 1 + late, n_all - 1))
+        each(
+            lambda peer: both(first(peer), both(~early, ~beside(peer))),
+            greet(far_sem),
+        )
+
+    @pl.when(last)
+    def _():
+        enter()
+
     landing = (x_in, z_in, y_in)
     leaving = (x_out, z_out, y_out)
     for (_, at, size), land in zip(places, landing):
@@ -173,6 +226,30 @@
     for r in range(rows):
         gathered[me * rows + r] = emitted[:, r * zone : (r + 1) * zone]
 
+    def push(start, length, peer, stage):
+        block = gathered.at[pl.ds(start, length)]
+        pltpu.make_async_remote_copy(
+            src_ref=block,
+            dst_ref=block,
+            send_sem=send_sem.at[stage],
+            recv_sem=recv_sem.at[stage],
+            device_id=peer,
+            device_id_type=MESH,
+        ).start()
+
+    def settle(length, sem):
+        block = gathered.at[pl.ds(0, length)]
+        pltpu.make_async_copy(block, block, sem).wait()
+
+    @pl.when(~last)
+    def _():
+        enter()
+
+    each(
+        lambda peer: both(other(peer), either(~early, first(peer))),
+        lambda peer: push(me * rows, rows, peer, 0),
+    )
+
     lane = iota((cells, cx), 1)
     packed = jnp.zeros((cells, cx), jnp.float32)
     for f in range(4):
@@ -183,25 +260,6 @@
         y_out[1, f] = field[pl.ds(cy - 1, cz, stride=cy), :]
         packed = jnp.where((lane >> 1) == f, pltpu.roll(field[...], 2 * f + 1, 1), packed)
     x_out[...] = jnp.transpose(packed)[:8]
-
-    pl.semaphore_wait(barrier, n_all - 1)
-
-    def push(start, length, peer, stage):
-        block = gathered.at[pl.ds(start, length)]
-        pltpu.make_async_remote_copy(
-            src_ref=block,
-            dst_ref=block,
-            send_sem=send_sem.at[stage],
-            recv_sem=recv_sem.at[stage],
-            device_id=peer,
-            device_id_type=MESH,
-        ).start()
-
-    def settle(length, sem):
-        block = gathered.at[pl.ds(0, length)]
-        pltpu.make_async_copy(block, block, sem).wait()
-
-    each(lambda peer: push(me * rows, rows, peer, 0))
 
     def face(which, side):
         axis, at, _ = places[which]
@@ -219,12 +277,15 @@
         _, at, size = places[which]
         return at > 0 if side == 0 else at < size - 1
 
-    for which in (1, 2, 0):
-        for side in (0, 1):
+    def launch(side):
+        for which in (1, 2, 0):
 
             @pl.when(has(which, side))
-            def _(which=which, side=side):
+            def _(which=which):
                 face(which, side).start()
+
+    launch(0)
+    launch(1)
 
     mean_out[...] = group_sum(group_sum(slabs, 0), 1)
     place = iota((cells, cx), 0)
@@ -238,6 +299,11 @@
         total += jnp.where(lane > 0, pltpu.roll(value, 1, 1), 0.0)
         total += jnp.where(lane < cx - 1, pltpu.roll(value, cx - 1, 1), 0.0)
         done[f] = value + diffusion_rates[f] * (total - 6.0 * value)
+
+    @pl.when(early)
+    def _():
+        pl.semaphore_wait(far_sem, n_all - n_first - late)
+        each(lambda peer: ~first(peer), lambda peer: push(me * rows, rows, peer, 0))
 
     for which in (0, 1, 2):
         for side in (0, 1):
@@ -373,8 +439,9 @@
                 pltpu.SemaphoreType.DMA((8,)),
                 pltpu.SemaphoreType.DMA((3, 2)),
                 pltpu.SemaphoreType.DMA((3, 2)),
-                pltpu.SemaphoreType.DMA((2,)),
-                pltpu.SemaphoreType.DMA((2,)),
+                pltpu.SemaphoreType.DMA((1,)),
+                pltpu.SemaphoreType.DMA((1,)),
+                pltpu.SemaphoreType.REGULAR,
             ],
             compiler_params=pltpu.CompilerParams(collective_id=0, has_side_effects=True),
         )(*flat, order, tiles, live, matrix)

time: 13 us -> 12.2 us (0.938)
  Pallas kernels: 12.2 us -> 11.4 us
    pallas_call x1, Pallas kernels: 10.9 us -> 10.1 us  [local(): pl.pallas_call(functools.partial(kernel, dims, counts), out_shape=[pltpu....]
where the time goes in v2:
time: 12.2 us; the launch traced here: 12.1 us
  Pallas kernels  11.4 us (93%)
  between operations  0.64 us (5%)
    pallas_call x1, Pallas kernels, local(): pl.pallas_call(functools.partial(kernel, dims, counts), out_shape=[pltpu....  10.1 us
    pallas_call x1, Pallas kernels, local(): pl.pallas_call(functools.partial(finish, dims), out_shape=[jax.ShapeDtype...  1.37 us

profile of v2, /device:TPU:0, one launch (start us, length us, event | category | flops | bytes accessed | tf_op | source)
XLA Modules:
  0.0 12.1 jit_solution(10993537261194284558)
XLA Ops:
  0.6 10.1 %shard_map.119 = (f32[4,256,128]{2,1,0:T(8,128)S(1)}, bf16[2,5,256,256]{3,2,1,0:T(8,128)(2,1)S(1)}, f32[2,5,1,256]{3,2,1,0:T(1,128)S(1)}, f32[64,128]{1,0:T(8,12...) custom-call(f32[256,128]{1,0:T(8,128)} %bitcast.10, f32[256,128]{1,0:T(8,128)} %bitcast.11, ...), custom_call_target="tpu_custom_call" | custom-call | tf_op jit(solution)/shard_map/pallas_call | solution.py:415
  10.7 1.4 %shard_map.120 = (f32[256,128]{1,0:T(8,128)}, f32[256,128]{1,0:T(8,128)}, f32[256,128]{1,0:T(8,128)}, f32[256,128]{1,0:T(8,128)}, f32[256,128]{1,0:T(8,128)}) custom-call(f32[4,256,128]{2,1,0:T(8,128)S(1)} %get-tuple-element.16.swept, bf16[2,5,256,256]{3,2,1,0:T(8,128)(2,1)S(1)} %get-tuple-element.17.matrix, f32[2,5,1,256]{3,2,1,0:T(1,128)S(1)} %get-tuple-element.18.picked, ...), custom_call_target="tpu_custom_call" | custom-call | tf_op jit(solution)/shard_map/pallas_call | solution.py:448

commit v3 on v2

--- a/solution.py
+++ b/solution.py
@@ -24,7 +24,7 @@
 VAPOUR_SLOPE = sum(c * k for c, k in zip(mixture_share_slope, vapour_attenuation_rate))
 
 MESH = pl.DeviceIdType.MESH
-NT = (((1,), (1,)), ((), ()))
+NN = (((1,), (0,)), ((), ()))
 TN = (((0,), (0,)), ((), ()))
 
 
@@ -55,10 +55,11 @@
     matrix_hbm,
     *rest,
 ):
-    done, matrix, picked_out, mean_out, rows_out, spread_out = rest[:6]
+    done, flipped, picked_out, mean_out, rows_out, spread_out = rest[:6]
     (
         fields,
         order_ref,
+        matrix,
         gathered,
         z_out,
         y_out,
@@ -68,7 +69,8 @@
         x_in,
         tile_ref,
         live_ref,
-        in_sem,
+        field_sem,
+        small_sem,
         face_send,
         face_recv,
         send_sem,
@@ -88,16 +90,16 @@
     me = sec * n_plane + plane
     n_all = n_sec * n_plane
 
-    copies = [
-        pltpu.make_async_copy(src, fields.at[i], in_sem.at[i])
-        for i, src in enumerate((kelvin_hbm, co2_hbm, h2o_hbm, soot_hbm))
-    ]
-    copies.append(pltpu.make_async_copy(order_hbm, order_ref, in_sem.at[4]))
-    copies.append(pltpu.make_async_copy(matrix_hbm, matrix, in_sem.at[5]))
-    copies.append(pltpu.make_async_copy(tile_hbm, tile_ref, in_sem.at[6]))
-    copies.append(pltpu.make_async_copy(live_hbm, live_ref, in_sem.at[7]))
-    for copy in copies[:5] + copies[6:]:
-        copy.start()
+    n_slab = cz // BOX
+    slab = BOX * cy
+    pltpu.make_async_copy(order_hbm, order_ref, small_sem.at[0]).start()
+    for t in range(n_slab):
+        part = pl.ds(t * slab, slab)
+        for i, src in enumerate((kelvin_hbm, co2_hbm, h2o_hbm, soot_hbm)):
+            pltpu.make_async_copy(src.at[part], fields.at[i, part], field_sem.at[0]).start()
+
+    def settle(ref, sem):
+        pltpu.make_async_copy(ref, ref, sem).wait()
 
     level = n_sec * n_blk
 
@@ -188,8 +190,10 @@
             def _(land=land, side=side):
                 land[side] = jnp.zeros(land.shape[1:], land.dtype)
 
-    copies[4].wait()
+    settle(order_ref, small_sem.at[0])
     order = order_ref[...]
+    tile_copy = pltpu.make_async_copy(tile_hbm, tile_ref, small_sem.at[0])
+    tile_copy.start()
     across = cx // BOX
     x_shape = (cx, zones)
     r_shape = (cells // BOX, zones)
@@ -199,30 +203,37 @@
     box_row = lax.div(r_at, cy) * (cy // BOX) + lax.div(lax.rem(r_at, cy), BOX)
     same_r = lax.div(order, across) == box_row
     spread_x = jnp.where(same_x, 1.0, 0.0).astype(jnp.bfloat16)
-    spread_out[...] = spread_x
     rows_out[...] = jnp.where(same_r, 1.0, 0.0)
-    for copy in copies[:4]:
-        copy.wait()
-    copies[5].start()
-
-    kelvin = fields[0]
-    vapour = fields[1] + fields[2]
-    soot_kelvin = fields[3] * kelvin
-    share = vapour * (VAPOUR_OFFSET + VAPOUR_SLOPE * kelvin) + (
-        particulate_attenuation_rate * soot_kelvin * (SHARE_OFFSET + SHARE_SLOPE * kelvin)
-    )
-    squared = kelvin * kelvin
-    emission = radiance_multiplier * (squared * squared) * share
-    slabs = emission.reshape(cz // BOX, BOX, cy, cx)
-    slabs = (slabs[:, 0] + slabs[:, 1] + slabs[:, 2] + slabs[:, 3]).reshape(cells // BOX, cx)
-    slabs = slabs * (1.0 / (BOX * BOX * BOX))
-    upper = slabs.astype(jnp.bfloat16)
-    lower = (slabs - upper.astype(jnp.float32)).astype(jnp.bfloat16)
+    total = jnp.zeros((cy, zones), jnp.float32)
+    means = []
+    settle(fields, field_sem.at[0])
+    matrix_copy = pltpu.make_async_copy(matrix_hbm, matrix, field_sem.at[0])
+    matrix_copy.start()
+    halves = []
+    for t in range(n_slab):
+        kelvin, co2, h2o, soot = (fields[i, pl.ds(t * slab, slab), :] for i in range(4))
+        vapour = co2 + h2o
+        soot_kelvin = soot * kelvin
+        share = vapour * (VAPOUR_OFFSET + VAPOUR_SLOPE * kelvin) + (
+            particulate_attenuation_rate * soot_kelvin * (SHARE_OFFSET + SHARE_SLOPE * kelvin)
+        )
+        squared = kelvin * kelvin
+        emission = (radiance_multiplier / BOX**3) * (squared * squared) * share
+        emission = emission.reshape(BOX, cy, cx)
+        mean = emission[0] + emission[1] + emission[2] + emission[3]
+        means.append(mean)
+        upper = mean.astype(jnp.bfloat16).astype(jnp.float32)
+        halves += [upper, mean - upper]
     by_row = jnp.dot(
-        jnp.concatenate([upper, lower], axis=0), spread_x, preferred_element_type=jnp.float32
-    )
-    by_row = by_row[: cells // BOX] + by_row[cells // BOX :]
-    emitted = jnp.sum(jnp.where(same_r, by_row, 0.0), axis=0, keepdims=True)
+        jnp.concatenate(halves, axis=0).astype(jnp.bfloat16),
+        spread_x,
+        preferred_element_type=jnp.float32,
+    )
+    for t in range(n_slab):
+        part = by_row[2 * t * cy : (2 * t + 1) * cy] + by_row[(2 * t + 1) * cy : (2 * t + 2) * cy]
+        total += jnp.where(same_r[t * cy : (t + 1) * cy], part, 0.0)
+    slabs = jnp.concatenate(means, axis=0)
+    emitted = jnp.sum(total, axis=0, keepdims=True)
     for r in range(rows):
         gathered[me * rows + r] = emitted[:, r * zone : (r + 1) * zone]
 
@@ -237,10 +248,6 @@
             device_id_type=MESH,
         ).start()
 
-    def settle(length, sem):
-        block = gathered.at[pl.ds(0, length)]
-        pltpu.make_async_copy(block, block, sem).wait()
-
     @pl.when(~last)
     def _():
         enter()
@@ -267,8 +274,8 @@
         return pltpu.make_async_remote_copy(
             src_ref=source,
             dst_ref=landing[which].at[1 - side],
-            send_sem=face_send.at[which, side],
-            recv_sem=face_recv.at[which, 1 - side],
+            send_sem=face_send.at[which],
+            recv_sem=face_recv.at[which],
             device_id={axis: at + (2 * side - 1)},
             device_id_type=MESH,
         )
@@ -276,6 +283,19 @@
     def has(which, side):
         _, at, size = places[which]
         return at > 0 if side == 0 else at < size - 1
+
+    def finish_faces(sem):
+        for which in (0, 1, 2):
+            low, high = has(which, 0), has(which, 1)
+            land = landing[which]
+
+            @pl.when(both(low, high))
+            def _(which=which, land=land):
+                settle(land, sem.at[which])
+
+            @pl.when(low != high)
+            def _(which=which, land=land):
+                settle(land.at[0], sem.at[which])
 
     def launch(side):
         for which in (1, 2, 0):
@@ -300,17 +320,23 @@
         total += jnp.where(lane < cx - 1, pltpu.roll(value, cx - 1, 1), 0.0)
         done[f] = value + diffusion_rates[f] * (total - 6.0 * value)
 
+    spread_out[...] = jnp.transpose(jnp.where(same_x, 1.0, 0.0)).astype(jnp.bfloat16)
+    tile_copy.wait()
+    live_copy = pltpu.make_async_copy(live_hbm, live_ref, small_sem.at[0])
+    live_copy.start()
+    matrix_copy.wait()
+
+    @pl.loop(0, rows * slots)
+    def _(i):
+        r, k = lax.div(i, slots), lax.rem(i, slots)
+        flipped[r, k] = jnp.transpose(matrix[r, k].astype(jnp.float32)).astype(jnp.bfloat16)
+
     @pl.when(early)
     def _():
         pl.semaphore_wait(far_sem, n_all - n_first - late)
         each(lambda peer: ~first(peer), lambda peer: push(me * rows, rows, peer, 0))
 
-    for which in (0, 1, 2):
-        for side in (0, 1):
-
-            @pl.when(has(which, side))
-            def _(which=which, side=side):
-                face(which, 1 - side).wait_recv()
+    finish_faces(face_recv)
 
     shape = (32, 4 * cx)
     row, column = iota(shape, 0) & 15, iota(shape, 1)
@@ -334,37 +360,25 @@
         out[pl.ds(0, cz, stride=cy), :] += rate * y_in[0, f]
         out[pl.ds(cy - 1, cz, stride=cy), :] += rate * y_in[1, f]
 
-    for copy in copies[5:]:
-        copy.wait()
-    settle((n_all - 1) * rows, recv_sem.at[0])
+    live_copy.wait()
+    settle(gathered.at[pl.ds(0, (n_all - 1) * rows)], recv_sem.at[0])
 
     for r in range(rows):
         for k in range(slots):
             tile = jnp.clip(tile_ref[r, k], 0, gathered.shape[0] - 1)
             picked_out[r, k] = jnp.where(k < live_ref[r], gathered[tile], 0.0)
 
-    settle((n_all - 1) * rows, send_sem.at[0])
-    for which in (0, 1, 2):
-        for side in (0, 1):
-
-            @pl.when(has(which, side))
-            def _(which=which, side=side):
-                face(which, side).wait_send()
-
-
-def finish(dims, swept, matrix, picked, box_mean, same_r, spread_x, *rest):
-    outs, heated, source_ref, sem = rest[:5], rest[5], rest[6], rest[7]
+    settle(gathered.at[pl.ds(0, (n_all - 1) * rows)], send_sem.at[0])
+    finish_faces(face_send)
+
+
+def finish(dims, swept, flipped, picked, box_mean, same_r, spread_x, *rest):
+    outs, final, sem = rest[:5], rest[5], rest[6]
     cz, cy, cx = dims
     cells = cz * cy
-    rows, slots, zone, _ = matrix.shape
-    copies = [
-        pltpu.make_async_copy(source, out, sem.at[i])
-        for i, (source, out) in enumerate(
-            zip((heated, swept.at[1], swept.at[2], swept.at[3], source_ref), outs)
-        )
-    ]
-    for copy in copies[1:4]:
-        copy.start()
+    rows, slots, zone, _ = flipped.shape
+    for i in (1, 2, 3):
+        pltpu.make_async_copy(swept.at[i], outs[i], sem.at[0]).start()
 
     absorbed = []
     for r in range(rows):
@@ -372,8 +386,8 @@
         for k in range(slots):
             total += lax.dot_general(
                 picked[r, k].astype(jnp.bfloat16),
-                matrix[r, k],
-                NT,
+                flipped[r, k],
+                NN,
                 preferred_element_type=jnp.float32,
             )
         absorbed.append(total)
@@ -382,17 +396,17 @@
     low = absorbed - high
     mask = same_r[...]
     both = jnp.concatenate([mask * high, mask * low], axis=0).astype(jnp.bfloat16)
-    carried = lax.dot_general(both, spread_x[...], NT, preferred_element_type=jnp.float32)
+    carried = lax.dot_general(both, spread_x[...], NN, preferred_element_type=jnp.float32)
     net = carried[: cells // BOX] + carried[cells // BOX :] - box_mean[...]
     source = jnp.broadcast_to(
         net.reshape(cz // BOX, 1, cy, cx), (cz // BOX, BOX, cy, cx)
     ).reshape(cells, cx)
-    source_ref[...] = source
-    copies[4].start()
-    heated[...] = swept[0] + heating_rate * source
-    copies[0].start()
-    for copy in copies:
-        copy.wait()
+    final[0] = source
+    pltpu.make_async_copy(final.at[0], outs[4], sem.at[1]).start()
+    final[1] = swept[0] + heating_rate * source
+    pltpu.make_async_copy(final.at[1], outs[0], sem.at[1]).start()
+    for ref, i in ((swept.at[pl.ds(1, 3)], 0), (final, 1)):
+        pltpu.make_async_copy(ref, ref, sem.at[i]).wait()
 
 
 def solution(mesh):
@@ -420,13 +434,14 @@
                 pltpu.VMEM((rows, slots, 1, zone), f32),
                 pltpu.VMEM((cells // BOX, cx), f32),
                 pltpu.VMEM((cells // BOX, zones), f32),
-                pltpu.VMEM((cx, zones), jnp.bfloat16),
+                pltpu.VMEM((zones, cx), jnp.bfloat16),
             ],
             in_specs=[anywhere] * 8,
             out_specs=[vmem] * 6,
             scratch_shapes=[
                 pltpu.VMEM((4, cells, cx), f32),
                 pltpu.VMEM(order.shape, jnp.int32),
+                pltpu.VMEM(matrix.shape, matrix.dtype),
                 pltpu.VMEM((blocks, 1, zone), f32),
                 pltpu.VMEM((2, 4, cy, cx), f32),
                 pltpu.VMEM((2, 4, cz, cx), f32),
@@ -436,9 +451,10 @@
                 pltpu.VMEM((2, 8, cells), f32),
                 pltpu.SMEM(tiles.shape, tiles.dtype),
                 pltpu.SMEM(live.shape, live.dtype),
-                pltpu.SemaphoreType.DMA((8,)),
-                pltpu.SemaphoreType.DMA((3, 2)),
-                pltpu.SemaphoreType.DMA((3, 2)),
+                pltpu.SemaphoreType.DMA((1,)),
+                pltpu.SemaphoreType.DMA((1,)),
+                pltpu.SemaphoreType.DMA((3,)),
+                pltpu.SemaphoreType.DMA((3,)),
                 pltpu.SemaphoreType.DMA((1,)),
                 pltpu.SemaphoreType.DMA((1,)),
                 pltpu.SemaphoreType.REGULAR,
@@ -451,9 +467,8 @@
             in_specs=[vmem] * 6,
             out_specs=[anywhere] * 5,
             scratch_shapes=[
-                pltpu.VMEM((cells, cx), f32),
-                pltpu.VMEM((cells, cx), f32),
-                pltpu.SemaphoreType.DMA((5,)),
+                pltpu.VMEM((2, cells, cx), f32),
+                pltpu.SemaphoreType.DMA((2,)),
             ],
             compiler_params=pltpu.CompilerParams(vmem_limit_bytes=16 << 20),
         )(*parts)

time: 12.2 us -> 11.9 us (0.975)
  Pallas kernels: 11.4 us -> 11 us
    pallas_call x1, Pallas kernels: 10.1 us -> 9.86 us  [local(): pl.pallas_call(functools.partial(kernel, dims, counts), out_shape=[pltpu....]
    pallas_call x1, Pallas kernels: 1.37 us -> 1.17 us  [local(): pl.pallas_call(functools.partial(finish, dims), out_shape=[jax.ShapeDtype...]
where the time goes in v3:
time: 11.9 us; the launch traced here: 11.7 us
  Pallas kernels  11 us (92%)
  between operations  0.64 us (5%)
    pallas_call x1, Pallas kernels, local(): pl.pallas_call(functools.partial(kernel, dims, counts), out_shape=[pltpu....  9.86 us
    pallas_call x1, Pallas kernels, local(): pl.pallas_call(functools.partial(finish, dims), out_shape=[jax.ShapeDtype...  1.17 us

profile of v3, /device:TPU:0, one launch (start us, length us, event | category | flops | bytes accessed | tf_op | source)
XLA Modules:
  0.0 11.7 jit_solution(5111169199901761164)
XLA Ops:
  0.6 9.9 %shard_map.119 = (f32[4,256,128]{2,1,0:T(8,128)S(1)}, bf16[2,5,256,256]{3,2,1,0:T(8,128)(2,1)S(1)}, f32[2,5,1,256]{3,2,1,0:T(1,128)S(1)}, f32[64,128]{1,0:T(8,12...) custom-call(f32[256,128]{1,0:T(8,128)} %bitcast.10, f32[256,128]{1,0:T(8,128)} %bitcast.11, ...), custom_call_target="tpu_custom_call" | custom-call | tf_op jit(solution)/shard_map/pallas_call | solution.py:429
  10.5 1.2 %shard_map.120 = (f32[256,128]{1,0:T(8,128)}, f32[256,128]{1,0:T(8,128)}, f32[256,128]{1,0:T(8,128)}, f32[256,128]{1,0:T(8,128)}, f32[256,128]{1,0:T(8,128)}) custom-call(f32[4,256,128]{2,1,0:T(8,128)S(1)} %get-tuple-element.16.swept, bf16[2,5,256,256]{3,2,1,0:T(8,128)(2,1)S(1)} %get-tuple-element.17.flipped, f32[2,5,1,256]{3,2,1,0:T(1,128)S(1)} %get-tuple-element.18.picked, ...), custom_call_target="tpu_custom_call" | custom-call | tf_op jit(solution)/shard_map/pallas_call | solution.py:464
